TPU v7x, 256 devices: a whole 4x4x8 slice. The times are simulated.
256 devices in a mesh: dp: 64 (over z, y_hi, x), mp: 4 (over y_lo, core).
Axes of the slice: x: 4, y: 4 (y_hi: 2, y_lo: 2; y = y_hi * 2 + y_lo), z: 8, core: 2. Of those that a mesh axis runs over, the one named last changes fastest.
Arguments:
- hidden: bfloat16 [65536, 4608], P('dp', 'mp'), may hold values from -6 to 6
- out_grad: bfloat16 [65536, 2304], P(('dp', 'mp')), may hold values from -0.1875 to 0.1875
- momentum: bfloat16 [147456, 4608], P('dp', 'mp'), may hold values from -6 to 6
Outputs:
- fresh_momentum: bfloat16 [147456, 4608], P('dp', 'mp')
- update: bfloat16 [2304, 4608], P('dp', 'mp')
All inputs are finite; a program needn't handle non-finite values.
Results may differ from a plain program's by a relative error of at most 0.003.
Values may be sent and summed in bfloat16 or wider, within the bound.
A program may use at most 192 MiB of HBM per device.

v0:
```python
import jax
import jax.numpy as jnp
from jax import lax
from jax.sharding import PartitionSpec as P

GROUP = 64
BAND = 16


DECAY = 0.9
highest = lax.Precision.HIGHEST


def dct_entry(frequency, position):
    norm_scale = jnp.where(frequency == 0, jnp.sqrt(1.0 / GROUP), jnp.sqrt(2.0 / GROUP))
    return norm_scale * jnp.cos(jnp.pi * (2.0 * position + 1.0) * frequency / (2.0 * GROUP))


def band_table():
    frequency = jnp.arange(BAND, dtype=jnp.float32)[:, None]
    position = jnp.arange(GROUP, dtype=jnp.float32)[None, :]
    return dct_entry(frequency, position)


def moment_rows(gathered, hidden, momentum):
    gradient = lax.dot_general(
        gathered, hidden, (((0,), (0,)), ((), ())), preferred_element_type=jnp.float32
    )
    return DECAY * momentum.astype(jnp.float32) + gradient


def forward_band(moment, band_tab):
    row_total, col_total = moment.shape
    blocks = moment.reshape(row_total // GROUP, GROUP, col_total // GROUP, GROUP)
    lefted = jnp.einsum("ai,ricj->racj", band_tab, blocks, precision=highest)
    return jnp.einsum("racj,bj->racb", lefted, band_tab, precision=highest)


def local_residual(moment, band_coef, band_tab):
    row_total, col_total = moment.shape
    righted = jnp.einsum("racb,bj->racj", band_coef, band_tab, precision=highest)
    restored = jnp.einsum("ai,racj->ricj", band_tab, righted, precision=highest)
    return (moment - restored.reshape(row_total, col_total)).astype(jnp.bfloat16)


def own_rows(summed, band_tab):
    share_rows = summed.shape[0] * GROUP // lax.axis_size("dp")
    first_row = lax.axis_index("dp") * share_rows
    positions = first_row + jnp.arange(share_rows, dtype=jnp.int32)
    picked = jnp.take(summed, positions // GROUP, axis=0)
    frequency = jnp.arange(BAND, dtype=jnp.float32)[None, :]
    weights = dct_entry(frequency, (positions % GROUP).astype(jnp.float32)[:, None])
    lefted = jnp.einsum("ra,racb->rcb", weights, picked, precision=highest)
    restored = jnp.einsum("rcb,bj->rcj", lefted, band_tab, precision=highest)
    return restored.reshape(share_rows, summed.shape[2] * GROUP)


def body(hidden, out_grad, momentum):
    gathered = lax.all_gather(out_grad, "mp", axis=0, tiled=True)
    band_tab = band_table()
    moment = moment_rows(gathered, hidden, momentum)
    band_coef = forward_band(moment, band_tab)
    summed = lax.psum(band_coef, "dp")
    fresh_mom = local_residual(moment, band_coef, band_tab)
    update = own_rows(summed, band_tab)
    return (fresh_mom, update.astype(jnp.bfloat16))


def solution(mesh):
    return jax.shard_map(
        body,
        mesh=mesh,
        in_specs=(P("dp", "mp"), P(("dp", "mp"), None), P("dp", "mp")),
        out_specs=(P("dp", "mp"), P("dp", "mp")),
        check_vma=False,
    )
```

profile of v0, /device:TPU:8, one launch (start us, length us, event | category | flops | bytes accessed | tf_op | source)
XLA Modules:
  0.0 956.6 jit_solution(12987492463191431749)
XLA Ops:
  7.2 0.0 copy-start
  7.2 0.0 all-gather.2.cloned.1.call-start
  7.2 0.7 all-gather.2.cloned.1.call-update
  8.0 0.2 multiply_bitcast_fusion
  8.2 56.3 %all-gather.2.cloned.1.call-done = bf16[1024,2304]{1,0:T(8,128)(2,1)} async-done(((bf16[256,2304]{1,0:T(8,128)(2,1)}), bf16[1024,2304]{1,0:T(8,128)(2,1)}) %all-gather.2.cloned.1.call-update) | async-done | bytes 4718608 | tf_op jit(solution)/shard_map/all_gather | solution.py:59
  64.5 0.0 copy-done
  64.5 11.3 %convolution_add_fusion = f32[2304,1152]{1,0:T(8,128)} fusion(bf16[1024,2304]{1,0:T(8,128)(2,1)} %all-gather.2.cloned.1.call-done, bf16[1024,1152]{1,0:T(8,128)(2,1)S(1)} %copy-done, bf16[2304,1152]{1,0:T(8,128)(2,1)} %param.5), kind=kOutput, calls=%fused_computation.1 | convolution fusion | flops 5443780608 | bytes 23003136 | tf_op jit(solution)/shard_map/dot_general | solution.py:26
  75.8 12.7 %copy.6 = f32[2304,1152]{0,1:T(8,128)} copy(f32[2304,1152]{1,0:T(8,128)} %convolution_add_fusion) | data formatting | bytes 21233664 | tf_op jit(solution)/shard_map/add | solution.py:29
  88.5 18.0 %reshape.121 = f32[36,64,18,64]{1,0,3,2:T(8,128)} reshape(f32[2304,1152]{0,1:T(8,128)} %copy.6) | data formatting | bytes 21233664 | tf_op jit(solution)/shard_map/reshape | solution.py:34
  106.5 81.5 %fusion.11 = f32[36,18,64,16]{0,3,2,1:T(8,128)} fusion(f32[36,64,18,64]{1,0,3,2:T(8,128)} %reshape.121, f32[64]{0:T(128)S(1)} %add_multiply_fusion, f32[16]{0:T(128)S(1)} %compare_select_fusion.2), kind=kOutput, calls=%fused_computation.18 | convolution fusion | flops 509611008 | bytes 13271360 | tf_op jit(solution)/shard_map/ai,ricj->racj/dot_general | solution.py:35
  188.0 8.8 copy.12
  196.8 21.7 %fusion = f32[36,16,18,16]{0,3,2,1:T(8,128)S(1)} fusion(f32[36,18,64,16]{2,0,1,3:T(8,128)} %copy.12, f32[64]{0:T(128)S(1)} %add_multiply_fusion, f32[16]{0:T(128)S(1)} %compare_select_fusion.2), kind=kOutput, calls=%fused_computation.4 | convolution fusion | flops 127405056 | bytes 3318080 | tf_op jit(solution)/shard_map/racj,bj->racb/dot_general | solution.py:36
  218.5 0.0 copy-start.2
  218.6 11.3 %fusion.8 = f32[36,16,18,64]{3,0,2,1:T(8,128)} fusion(f32[36,16,18,16]{0,3,2,1:T(8,128)S(1)} %fusion, f32[64]{0:T(128)S(1)} %add_multiply_fusion, f32[16]{0:T(128)S(1)} %compare_select_fusion.2), kind=kOutput, calls=%fused_computation.15 | convolution fusion | flops 127405056 | bytes 3318080 | tf_op jit(solution)/shard_map/racb,bj->racj/dot_general | solution.py:41
  229.8 0.0 all-reduce.2.cloned.1.call-start
  229.8 0.0 copy-done.2
  229.8 0.7 all-reduce.2.cloned.1.call-update
  230.6 38.2 %convolution_bitcast_fusion = f32[36,64,18,64]{1,3,2,0:T(8,128)} fusion(f32[36,16,18,64]{3,0,2,1:T(8,128)} %fusion.8, f32[64]{0:T(128)S(1)} %add_multiply_fusion, f32[16]{0:T(128)S(1)} %compare_select_fusion.2), kind=kOutput, calls=%fused_computation.3 | convolution fusion | flops 509611008 | bytes 13271360 | tf_op jit(solution)/shard_map/ai,racj->ricj/dot_general | solution.py:42
  268.8 24.9 %copy.17 = f32[36,64,18,64]{3,2,1,0:T(8,128)} copy(f32[36,64,18,64]{1,3,2,0:T(8,128)} %convolution_bitcast_fusion) | data formatting | bytes 21233664 | tf_op jit(solution)/shard_map/reshape | solution.py:43
  293.7 20.5 %reshape.135 = f32[2304,1152]{1,0:T(8,128)} reshape(f32[36,64,18,64]{3,2,1,0:T(8,128)} %copy.17) | data formatting | bytes 21233664 | tf_op jit(solution)/shard_map/reshape | solution.py:43
  314.2 10.1 %subtract_convert_fusion = bf16[2304,1152]{1,0:T(8,128)(2,1)} fusion(f32[2304,1152]{1,0:T(8,128)} %convolution_add_fusion, f32[2304,1152]{1,0:T(8,128)} %reshape.135), kind=kLoop, calls=%fused_computation.2 | loop fusion | flops 5308416 | bytes 26542080 | tf_op jit(solution)/shard_map/convert_element_type | solution.py:43
  324.3 604.1 %all-reduce.2.cloned.1.call-done = f32[36,16,18,16]{0,3,2,1:T(8,128)} async-done(((f32[36,16,18,16]{0,3,2,1:T(8,128)}), f32[36,16,18,16]{0,3,2,1:T(8,128)}) %all-reduce.2.cloned.1.call-update) | async-done | bytes 663568 | tf_op jit(solution)/shard_map/psum | solution.py:63
  928.4 6.9 copy.9
  935.4 5.4 gather_fusion
  940.7 0.0 copy-start.1
  940.7 3.2 broadcast_select_fusion
  943.9 3.7 fusion.3
  947.6 0.2 copy.16
  947.8 0.8 convolution_convert_fusion
  948.7 0.8 convert_element_type.23
  949.5 0.0 copy-done.1
  (7 shorter events, 0.1 us)
Async XLA Ops:
  7.2 57.3 %copy-start = (bf16[1024,1152]{1,0:T(8,128)(2,1)S(1)}, bf16[1024,1152]{1,0:T(8,128)(2,1)}, u32[]{:S(2)}) copy-start(bf16[1024,1152]{1,0:T(8,128)(2,1)} %param.3) | copy-start | bytes 7077892
  7.2 57.3 %all-gather.2.cloned.1.call-start = ((), (), s32[]{:S(2)}) async-start(), calls=%async_computation | async-start | bytes 5898240 | tf_op jit(solution)/shard_map/all_gather | solution.py:59
  218.5 11.3 %copy-start.2 = (f32[36,16,18,16]{0,3,2,1:T(8,128)}, f32[36,16,18,16]{0,3,2,1:T(8,128)S(1)}, u32[]{:S(2)}) copy-start(f32[36,16,18,16]{0,3,2,1:T(8,128)S(1)} %fusion) | copy-start | bytes 1990660
  229.8 698.6 %all-reduce.2.cloned.1.call-start = ((), (), s32[]{:S(2)}) async-start(), calls=%async_computation.1 | async-start | bytes 4718592 | tf_op jit(solution)/shard_map/psum | solution.py:63
  940.7 8.8 copy-start.1
Sparse Core Ops, SparseCore 0:
  9.8 54.5 all-gather.1
  233.3 695.1 all-reduce.1
where the time goes:
time: 962 us; the launch traced here: 957 us
  waiting for transfers between devices  662 us (69%)
  matrix products  169 us (18%)
  local copies, waits for them, and re-layouts  98.3 us (10%)
  between operations  14.3 us (1%)
  other arithmetic  13.6 us (1%)
    psum x1, waiting for transfers between devices, body(): summed = lax.psum(band_coef, 'dp')  604 us
    dot_general x1, matrix products, forward_band(): lefted = jnp.einsum('ai,ricj->racj', band_tab, blocks, precision=highest)  81.5 us
    all_gather x1, waiting for transfers between devices, body(): gathered = lax.all_gather(out_grad, 'mp', axis=0, tiled=True)  56.3 us
    reshape x2, local copies, waits for them, and re-layouts, local_residual(): restored.reshape(row_total, col_total)  45.4 us
    dot_general x1, matrix products, local_residual(): restored = jnp.einsum('ai,racj->ricj', band_tab, righted, precision=highest)  38.2 us
    dot_general x1, matrix products, forward_band(): return jnp.einsum('racj,bj->racb', lefted, band_tab, precision=highest)  21.7 us
  transfers between devices with their start and end apart: 2, of which 2 were waited for; matrix products, arithmetic and copies ran while one was open for 10% of the time, Pallas kernels for 0%

commit v1 on v0

v1 whole, which is shorter than its diff:
```python
import jax
import jax.numpy as jnp
import ml_dtypes
import numpy as np
from jax import lax
from jax.experimental import pallas as pl
from jax.experimental.pallas import tpu as pltpu
from jax.sharding import PartitionSpec as P

MESH = pl.DeviceIdType.MESH
F32, BF16 = jnp.float32, jnp.bfloat16
GROUP, BAND, DECAY = 64, 16, 0.9
D_WIN, TOK, COLS = 2304, 1024, 1152
QTOK, HALF_TOK = 256, 512
NZ, NX, NDP = 8, 4, 64
SHARE = D_WIN // NDP
PADDED_SHARE = 40
BLOCKS = ((0, 512), (512, 512), (1024, 128))
BW = 384


def dct():
    k = np.arange(GROUP)[:, None].astype(np.float64)
    n = np.arange(GROUP)[None, :].astype(np.float64)
    scale = np.where(k == 0, np.sqrt(1.0 / GROUP), np.sqrt(2.0 / GROUP))
    return scale * np.cos(np.pi * (2.0 * n + 1.0) * k / (2.0 * GROUP))


def group_table(groups):
    c = dct()
    table = np.zeros((GROUP * groups, GROUP * groups))
    high = GROUP - BAND
    for g in range(groups):
        rows = slice(GROUP * g, GROUP * (g + 1))
        table[rows, BAND * g : BAND * (g + 1)] = c[:BAND].T
        first = BAND * groups + high * g
        table[rows, first : first + high] = c[BAND:].T
    return table


def halves(x):
    hi = x.astype(np.float32).astype(ml_dtypes.bfloat16)
    lo = (x - hi.astype(np.float64)).astype(np.float32).astype(ml_dtypes.bfloat16)
    return np.stack([hi, lo])


def share_table():
    c = dct()
    table = np.zeros((NDP, PADDED_SHARE, 2 * BAND), np.float32)
    for d in range(NDP):
        first = SHARE * d // GROUP
        for r in range(SHARE):
            pos = SHARE * d + r
            i = pos // GROUP - first
            table[d, r, BAND * i : BAND * (i + 1)] = c[:BAND, pos % GROUP]
    return table


def nn(a, b):
    return lax.dot_general(a, b, (((1,), (0,)), ((), ())), preferred_element_type=F32)


def tn(a, b):
    return lax.dot_general(a, b, (((0,), (0,)), ((), ())), preferred_element_type=F32)


def nt(a, b):
    return lax.dot_general(a, b, (((1,), (1,)), ((), ())), preferred_element_type=F32)


def split(x):
    hi = x.astype(BF16)
    return hi, (x - hi.astype(F32)).astype(BF16)


def three(op, a, b):
    return op(a[0], b[0]) + (op(a[1], b[0]) + op(a[0], b[1]))


def kernel(
    hid, og, mom, f8_in, f4_in, share_in,
    out, upd,
    f8, f4, share, og_all, h_all, mom_all, acc, wlo, whi, wh4, rlo, rhi, rh4,
    hp, band1, band, xr, xs, zr, zs, fin,
    l_sem, y_send, y_recv, f_send, f_recv, s_send, s_recv, x_send, x_recv, z_send, z_recv, fin_send, fin_recv,
):
    dp, mp = lax.axis_index("dp"), lax.axis_index("mp")
    z, h, x = dp // 8, (dp // 4) % 2, dp % 4
    l, c = mp // 2, mp % 2
    y_peer = (dp, (1 - l) * 2 + c)
    sib = (dp, l * 2 + 1 - c)
    x_peers = [(z * 8 + h * 4 + (x + o) % 4, mp) for o in range(1, 4)]
    z_peers = [(((z + o) % 8) * 8 + h * 4 + x, mp) for o in range(1, 8)]
    h_peer = (z * 8 + (1 - h) * 4 + x, mp)

    def rows(first, n, mult):
        return pl.ds(pl.multiple_of(first, mult), n)

    own = rows(mp * QTOK, QTOK, QTOK)
    yrows = rows(((1 - l) * 2 + c) * QTOK, QTOK, QTOK)
    loc = rows(l * HALF_TOK, HALF_TOK, HALF_TOK)
    rem = rows((1 - l) * HALF_TOK, HALF_TOK, HALF_TOK)

    def remote(src, dst, s, r, dev):
        return pltpu.make_async_remote_copy(
            src_ref=src, dst_ref=dst, send_sem=s, recv_sem=r, device_id=dev, device_id_type=MESH
        )

    loads = [
        pltpu.make_async_copy(og, og_all.at[own, :], l_sem.at[0]),
        pltpu.make_async_copy(f8_in, f8, l_sem.at[1]),
        pltpu.make_async_copy(f4_in, f4, l_sem.at[2]),
        pltpu.make_async_copy(hid, h_all, l_sem.at[3]),
        pltpu.make_async_copy(mom, mom_all, l_sem.at[4]),
        pltpu.make_async_copy(share_in.at[dp], share, l_sem.at[5]),
    ]
    for cp in loads:
        cp.start()
    fin[...] = jnp.zeros_like(fin)

    barrier = pltpu.get_barrier_semaphore()
    greeted = [y_peer, sib, h_peer] + x_peers + z_peers
    for dev in greeted:
        pl.semaphore_signal(barrier, inc=1, device_id=dev, device_id_type=MESH)
    loads[0].wait()
    loads[1].wait()
    loads[2].wait()
    for j in range(4):
        a = og_all[own, 512 * j : 512 * (j + 1)]
        wlo[j] = (nn(a, f8[0, :, 0:128]) + nn(a, f8[1, :, 0:128])).astype(BF16)
    a = og_all[own, 2048:2304]
    wlo[4] = (nn(a, f4[0, :, 0:128]) + nn(a, f4[1, :, 0:128])).astype(BF16)
    pl.semaphore_wait(barrier, len(greeted))

    sib_copy = remote(og, og_all.at[own, :], s_send, s_recv, sib)
    sib_copy.start()
    y_low = [remote(wlo.at[j], rlo.at[c, j], y_send.at[j], y_recv.at[j], y_peer) for j in range(5)]
    y_high = [remote(whi.at[k], rhi.at[k], y_send.at[5 + k], y_recv.at[5 + k], y_peer) for k in range(4)]
    y_high.append(remote(wh4, rh4, y_send.at[9], y_recv.at[9], y_peer))
    for cp in y_low:
        cp.start()
    for k in range(4):
        a = og_all[own, 512 * k : 512 * (k + 1)]
        whi[k] = (nn(a, f8[0, :, 128:512]) + nn(a, f8[1, :, 128:512])).astype(BF16)
        y_high[k].start()
    a = og_all[own, 2048:2304]
    wh4[...] = (nn(a, f4[0, :, 128:256]) + nn(a, f4[1, :, 128:256])).astype(BF16)
    y_high[4].start()

    loads[3].wait()
    loads[4].wait()
    sib_copy.wait_recv()

    def own_part(k, r0, n):
        for b, (c0, cn) in enumerate(BLOCKS):
            g = tn(og_all[loc, pl.ds(r0, n)], h_all[loc, c0 : c0 + cn])
            g = DECAY * mom_all[pl.ds(r0, n), c0 : c0 + cn].astype(F32) + g
            acc[pl.ds(r0, n), c0 : c0 + cn] = g
            left = three(tn, (f8[0, 0:n, 0:128], f8[1, 0:n, 0:128]), split(g))
            right = three(nn, split(left), (f8[0, 0:cn, 0:128], f8[1, 0:cn, 0:128]))
            band1[k, :, 128 * b : 128 * (b + 1)] = right

    def own_step(k, carry):
        own_part(k, pl.multiple_of(k * 512, 512), 512)
        return carry

    lax.fori_loop(0, 4, own_step, 0)
    own_part(4, 2048, 256)
    for b, (c0, cn) in enumerate(BLOCKS):
        a = h_all[rem, c0 : c0 + cn]
        p = nn(a, f8[0, 0:cn, 0:128]) + nn(a, f8[1, 0:cn, 0:128])
        hp[0, :, 128 * b : 128 * (b + 1)], hp[1, :, 128 * b : 128 * (b + 1)] = split(p)

    x_sends = []
    f_low = [remote(rlo.at[c, j], rlo.at[c, j], f_send.at[j], f_recv.at[j], sib) for j in range(5)]
    for j in range(5):
        y_low[j].wait_recv()
        f_low[j].start()
    for j in range(5):
        total = band1[j]
        f_low[j].wait_recv()
        for cc in range(2):
            w = rlo[cc, j]
            part = rows(cc * QTOK, QTOK, QTOK)
            total = total + (tn(w, hp[0, part, :]) + tn(w, hp[1, part, :]))
        band[j] = total
        n = 32 if j < 4 else 16
        for o in range(1, 4):
            theirs = rows(((x + o) % 4) * n, n, n)
            cp = remote(band.at[j, theirs, :], xr.at[j, o - 1, 0:n, :], x_send.at[j, o - 1], x_recv.at[j, o - 1], x_peers[o - 1])
            cp.start()
            x_sends.append(cp)

    def chunk(k, r0, n, high_ref, f):
        y_high[k].wait_recv()
        low, high = rlo[c, k], high_ref[...]
        ogy = nt(low, f[0, :, 0:128]) + nt(low, f[1, :, 0:128])
        ogy = ogy + (nt(high, f[0, :, 128:n]) + nt(high, f[1, :, 128:n]))
        og_all[yrows, r0 : r0 + n] = ogy.astype(BF16)
        there = og_all.at[yrows, r0 : r0 + n]
        fwd = remote(there, there, f_send.at[5 + k], f_recv.at[5 + k], sib)
        fwd.start()
        fwd.wait_recv()
        a = og_all[rem, r0 : r0 + n]
        ap = split(nn(a, f8[0, 0:n, 0:128]) + nn(a, f8[1, 0:n, 0:128]))
        for b, (c0, cn) in enumerate(BLOCKS):
            lanes = slice(128 * b, 128 * (b + 1))
            bandf = band1[k, :, lanes] + three(tn, ap, (hp[0, :, lanes], hp[1, :, lanes]))
            t1 = three(nt, split(bandf), (f8[0, 0:cn, 0:128], f8[1, 0:cn, 0:128]))
            restored = three(nn, (f8[0, 0:n, 0:128], f8[1, 0:n, 0:128]), split(t1))
            g = tn(a, h_all[rem, c0 : c0 + cn])
            out[r0 : r0 + n, c0 : c0 + cn] = (acc[r0 : r0 + n, c0 : c0 + cn] + g - restored).astype(BF16)
        return fwd

    forwards = list(f_low)
    forwards.append(chunk(0, 0, 512, rhi.at[0], f8))

    z_sends = []
    for j in range(5):
        n = 32 if j < 4 else 16
        for o in range(3):
            x_sends[3 * j + o].wait_recv()
        mine = rows(x * n, n, n)
        xs[j, 0:n, :] = band[j, mine, :] + xr[j, 0, 0:n, :] + xr[j, 1, 0:n, :] + xr[j, 2, 0:n, :]
        for q in range(n // 8):
            to = (4 * (j % 2) if j < 4 else 0) + q
            away = (to - z + 8) % 8
            cp = remote(
                xs.at[j, 8 * q : 8 * (q + 1), :],
                zr.at[j // 2, jnp.maximum(away - 1, 0)],
                z_send.at[j, q],
                z_recv.at[j // 2, jnp.maximum(away - 1, 0)],
                (to * 8 + h * 4 + x, mp),
            )
            z_sends.append((cp, away))

            @pl.when(away != 0)
            def _():
                cp.start()

    forwards.append(chunk(1, 512, 512, rhi.at[1], f8))
    forwards.append(chunk(2, 1024, 512, rhi.at[2], f8))

    fin_sends = []
    for t in range(3):
        j = z // 4 + 2 * t if t < 2 else 4
        q = z % 4 if t < 2 else z % 2
        group = 8 * j + 2 * x + q // 2 if t < 2 else 32 + x
        half = q % 2
        first, last = (64 * group) // 36, (64 * group + 63) // 36
        there = z < 2 if t == 2 else z >= 0

        @pl.when(there)
        def _():
            total = xs[j, rows(8 * q, 8, 8), :]
            for o in range(7):
                slot = zr.at[t, o]
                remote(slot, slot, z_send.at[0, 0], z_recv.at[t, o], z_peers[0]).wait_recv()
                total = total + zr[t, o]
            zs[t] = total

        for u in range(3):
            owner = jnp.minimum(first + u, NDP - 1)
            slot = (group - (36 * owner) // 64) * 2 + half
            slot = jnp.clip(slot, 0, 3)
            goes = there & (first + u <= last)
            cp = remote(zs.at[t], fin.at[h, slot], fin_send.at[t, u], fin_recv.at[h, slot], (owner, mp))
            at_home = pltpu.make_async_copy(zs.at[t], fin.at[h, slot], fin_recv.at[h, slot])
            fin_sends.append((cp, goes & (owner != dp)))

            @pl.when(goes & (owner != dp))
            def _():
                cp.start()

            @pl.when(goes & (owner == dp))
            def _():
                at_home.start()

    forwards.append(chunk(3, 1536, 512, rhi.at[3], f8))

    two = (36 * dp + 35) // 64 - (36 * dp) // 64
    for hh in range(2):
        for s in range(4):

            def arrived(hh=hh, s=s):
                slot = fin.at[hh, s]
                pltpu.make_async_copy(slot, slot, fin_recv.at[hh, s]).wait()

            if s < 2:
                arrived()
            else:
                pl.when(two == 1)(arrived)
    loads[5].wait()
    low = [fin[0, s] + fin[1, s] for s in range(4)]
    low = jnp.concatenate(low, axis=0)
    lefted = lax.dot_general(
        share[...], low, (((1,), (0,)), ((), ())), precision=lax.Precision.HIGHEST, preferred_element_type=F32
    )
    for b, (c0, cn) in enumerate(BLOCKS):
        u = three(nt, split(lefted[:, 128 * b : 128 * (b + 1)]), (f8[0, 0:cn, 0:128], f8[1, 0:cn, 0:128]))
        upd[:, c0 : c0 + cn] = u[0:SHARE].astype(BF16)

    forwards.append(chunk(4, 2048, 256, rh4, f4))

    sib_copy.wait_send()
    for cp in y_low + y_high + forwards + x_sends:
        cp.wait_send()
    for cp, away in z_sends:
        pl.when(away != 0)(cp.wait_send)
    for cp, goes in fin_sends:
        pl.when(goes)(cp.wait_send)


def body(hidden, out_grad, momentum):
    f8, f4 = halves(group_table(8)), halves(group_table(4))
    hbm = pl.BlockSpec(memory_space=pltpu.HBM)
    vmem = pl.BlockSpec(memory_space=pltpu.VMEM)
    dma = pltpu.SemaphoreType.DMA
    return pl.pallas_call(
        kernel,
        out_shape=(pltpu.VMEM((D_WIN, COLS), BF16), pltpu.VMEM((SHARE, COLS), BF16)),
        in_specs=[hbm] * 6,
        out_specs=(vmem, vmem),
        scratch_shapes=[
            pltpu.VMEM((2, 512, 512), BF16),
            pltpu.VMEM((2, 256, 256), BF16),
            pltpu.VMEM((PADDED_SHARE, 2 * BAND), F32),
            pltpu.VMEM((TOK, D_WIN), BF16),
            pltpu.VMEM((TOK, COLS), BF16),
            pltpu.VMEM((D_WIN, COLS), BF16),
            pltpu.VMEM((D_WIN, COLS), F32),
            pltpu.VMEM((5, QTOK, 128), BF16),
            pltpu.VMEM((4, QTOK, 384), BF16),
            pltpu.VMEM((QTOK, 128), BF16),
            pltpu.VMEM((2, 5, QTOK, 128), BF16),
            pltpu.VMEM((4, QTOK, 384), BF16),
            pltpu.VMEM((QTOK, 128), BF16),
            pltpu.VMEM((2, HALF_TOK, BW), BF16),
            pltpu.VMEM((5, 128, BW), F32),
            pltpu.VMEM((5, 128, BW), F32),
            pltpu.VMEM((5, 3, 32, BW), F32),
            pltpu.VMEM((5, 32, BW), F32),
            pltpu.VMEM((3, 7, 8, BW), F32),
            pltpu.VMEM((3, 8, BW), F32),
            pltpu.VMEM((2, 4, 8, BW), F32),
            dma((6,)), dma((10,)), dma((10,)), dma((10,)), dma((10,)), dma, dma,
            dma((5, 3)), dma((5, 3)), dma((5, 4)), dma((3, 7)), dma((3, 3)), dma((2, 4)),
        ],
        compiler_params=pltpu.CompilerParams(
            collective_id=0, has_side_effects=True, vmem_limit_bytes=54 * 2**20
        ),
        cost_estimate=pl.CostEstimate(flops=4 * 2 * TOK * D_WIN * COLS, bytes_accessed=16 * 2**20, transcendentals=0),
    )(hidden, out_grad, momentum, f8, f4, share_table())


def solution(mesh):
    return jax.shard_map(
        body,
        mesh=mesh,
        in_specs=(P("dp", "mp"), P(("dp", "mp"), None), P("dp", "mp")),
        out_specs=(P("dp", "mp"), P("dp", "mp")),
        check_vma=False,
    )
```

time: 962 us -> 66.5 us (0.07)
  the two profiles are of different devices: /device:TPU:8 before, /device:TPU:1 now
where the time goes in v1:
time: 66.5 us; the launch traced here: 65.9 us
  Pallas kernels  62.3 us (94%)
  local copies, waits for them, and re-layouts  3.02 us (5%)
    pallas_call x1, Pallas kernels, body(): pl.pallas_call(kernel, out_shape=(pltpu.VMEM((D_WIN, COLS), BF16), pltpu....  62.3 us
    unnamed x2, local copies, waits for them, and re-layouts  3.02 us

profile of v1, /device:TPU:1, one launch (start us, length us, event | category | flops | bytes accessed | tf_op | source)
XLA Modules:
  0.0 65.9 jit_solution(12259653220614667900)
XLA Ops:
  0.6 62.3 %shard_map.77 = (bf16[2304,1152]{1,0:T(8,128)(2,1)S(1)}, bf16[36,1152]{1,0:T(8,128)(2,1)S(1)}) custom-call(bf16[1024,1152]{1,0:T(8,128)(2,1)} %hid.1, bf16[256,2304]{1,0:T(8,128)(2,1)} %og.1, bf16[2304,1152]{1,0:T(8,128)(2,1)} %mom.1, bf16[2,512,512]{2,1,0:T(8,128)(2,1)} %constant.6.clone.f8_in, bf16[2,256,256]{2,1,0:T(8,128)(2,1)} %constant.7.clone.f4_in, ...), custom_call_target="tpu_custom_call" | custom-call | flops 21743271936 | bytes 16777216 | tf_op jit(solution)/shard_map/pallas_call | solution.py:319
  62.9 2.4 %copy.10 = bf16[2304,1152]{1,0:T(8,128)(2,1)} copy(bf16[2304,1152]{1,0:T(8,128)(2,1)S(1)} %get-tuple-element.2) | data formatting | bytes 10616832
  65.3 0.6 copy.11

commit v2 on v1

v2 whole, which is shorter than its diff:
```python
import jax
import jax.numpy as jnp
import ml_dtypes
import numpy as np
from jax import lax
from jax.experimental import pallas as pl
from jax.experimental.pallas import tpu as pltpu
from jax.sharding import PartitionSpec as P

MESH = pl.DeviceIdType.MESH
F32, BF16 = jnp.float32, jnp.bfloat16
GROUP, BAND, DECAY = 64, 16, 0.9
D_WIN, TOK, COLS = 2304, 1024, 1152
QTOK, HALF_TOK = 256, 512
NZ, NX, NDP = 8, 4, 64
SHARE = D_WIN // NDP
PADDED_SHARE = 40
BLOCKS = ((0, 512), (512, 512), (1024, 128))
BW = 384


def dct():
    k = np.arange(GROUP)[:, None].astype(np.float64)
    n = np.arange(GROUP)[None, :].astype(np.float64)
    scale = np.where(k == 0, np.sqrt(1.0 / GROUP), np.sqrt(2.0 / GROUP))
    return scale * np.cos(np.pi * (2.0 * n + 1.0) * k / (2.0 * GROUP))


def group_table(groups):
    c = dct()
    table = np.zeros((GROUP * groups, GROUP * groups))
    high = GROUP - BAND
    for g in range(groups):
        rows = slice(GROUP * g, GROUP * (g + 1))
        table[rows, BAND * g : BAND * (g + 1)] = c[:BAND].T
        first = BAND * groups + high * g
        table[rows, first : first + high] = c[BAND:].T
    return table


def halves(x):
    hi = x.astype(np.float32).astype(ml_dtypes.bfloat16)
    lo = (x - hi.astype(np.float64)).astype(np.float32).astype(ml_dtypes.bfloat16)
    return np.stack([hi, lo])


def share_table():
    c = dct()
    table = np.zeros((NDP, PADDED_SHARE, 2 * BAND), np.float32)
    for d in range(NDP):
        first = SHARE * d // GROUP
        for r in range(SHARE):
            pos = SHARE * d + r
            i = pos // GROUP - first
            table[d, r, BAND * i : BAND * (i + 1)] = c[:BAND, pos % GROUP]
    return table


def nn(a, b):
    return lax.dot_general(a, b, (((1,), (0,)), ((), ())), preferred_element_type=F32)


def tn(a, b):
    return lax.dot_general(a, b, (((0,), (0,)), ((), ())), preferred_element_type=F32)


def nt(a, b):
    return lax.dot_general(a, b, (((1,), (1,)), ((), ())), preferred_element_type=F32)


def split(x):
    hi = x.astype(BF16)
    return hi, (x - hi.astype(F32)).astype(BF16)


def cat(parts, axis):
    return jnp.concatenate(parts, axis=axis)


def fold(x, n):
    return x[:, 0:n] + x[:, n : 2 * n]


def stacked(x, axis):
    hi, lo = split(x)
    return cat((hi, lo, hi), axis)


def tables():
    f8, f4 = group_table(8), group_table(4)
    low8, low4 = halves(f8[:, 0:128]), halves(f4[:, 0:64])
    wide = lambda m: np.concatenate(list(halves(m)), axis=1)
    fl = np.concatenate(list(low8), axis=1)
    kts = np.concatenate([low8[0].T, low8[0].T, low8[1].T], axis=0)
    fts = -np.concatenate([low4[0].T, low4[1].T, low4[0].T], axis=0)
    return (
        fl, wide(f8[:, 128:512]), wide(f4[:, 0:128]), wide(f4[:, 128:256]),
        wide(f8.T), wide(f4.T), kts, fts, share_table(),
    )


def kernel(
    hid, og, mom, fl_in, fh_in, f4a_in, f4b_in, i8_in, i4_in, kts_in, fts_in, share_in,
    out, upd,
    fl, fh, f4a, f4b, i8, i4, kts, share, ogx, hx, ext, mom_all, wlo, whi, wh4, rlo, rhi, rh4,
    hp, band1, band, xr, xs, zr, zs, fin,
    l_sem, y_send, y_recv, f_send, f_recv, s_send, s_recv, x_send, x_recv, z_send, z_recv, fin_send, fin_recv, go, know,
):
    dp, mp = lax.axis_index("dp"), lax.axis_index("mp")
    z, h, x = dp // 8, (dp // 4) % 2, dp % 4
    l, c = mp // 2, mp % 2
    y_peer = (dp, (1 - l) * 2 + c)
    sib = (dp, l * 2 + 1 - c)
    diag = (dp, (1 - l) * 2 + 1 - c)
    x_peers = [(z * 8 + h * 4 + (x + o) % 4, mp) for o in range(1, 4)]
    z_peers = [(((z + o) % 8) * 8 + h * 4 + x, mp) for o in range(1, 8)]
    h_peer = (z * 8 + (1 - h) * 4 + x, mp)

    def rows(first, n, mult):
        return pl.ds(pl.multiple_of(first, mult), n)

    own = rows(mp * QTOK, QTOK, QTOK)
    yrows = rows(((1 - l) * 2 + c) * QTOK, QTOK, QTOK)
    loc = rows(l * HALF_TOK, HALF_TOK, HALF_TOK)
    rem = rows((1 - l) * HALF_TOK, HALF_TOK, HALF_TOK)
    mine_c = rows(c * QTOK, QTOK, QTOK)

    def remote(src, dst, s, r, dev):
        return pltpu.make_async_remote_copy(
            src_ref=src, dst_ref=dst, send_sem=s, recv_sem=r, device_id=dev, device_id_type=MESH
        )

    def signal(sem, dev):
        pl.semaphore_signal(sem, inc=1, device_id=dev, device_id_type=MESH)

    fin[...] = jnp.zeros_like(fin)

    barrier = pltpu.get_barrier_semaphore()
    for first_core in (0, 2):

        @pl.when(mp != first_core)
        def _():
            signal(barrier, (dp, first_core))

    pairs = [(og, ogx.at[own, :]), (fl_in, fl), (f4a_in, f4a), (fh_in, fh), (f4b_in, f4b), (hid, hx.at[0:TOK, :])]
    pairs += [(mom.at[512 * k : min(512 * (k + 1), D_WIN), :], mom_all.at[512 * k : min(512 * (k + 1), D_WIN), :]) for k in range(5)]
    pairs += [(i8_in, i8), (i4_in, i4), (kts_in, kts), (share_in.at[dp], share)]
    pairs += [(fts_in, ogx.at[TOK : TOK + 192, 256 * k : 256 * (k + 1)]) for k in range(9)]
    loads = [pltpu.make_async_copy(a, b, l_sem.at[i]) for i, (a, b) in enumerate(pairs)]
    for cp in loads[:3]:
        cp.start()

    @pl.when(c == 0)
    def _():
        pl.semaphore_wait(barrier, 3)
        signal(go, sib)

    sib_copy = remote(og, ogx.at[own, :], s_send, s_recv, sib)
    y_low = [remote(wlo.at[j], rlo.at[j, mine_c, :], y_send.at[j], y_recv.at[j], y_peer) for j in range(5)]
    y_high = [remote(whi.at[k], rhi.at[k], y_send.at[5 + k], y_recv.at[5 + k], y_peer) for k in range(4)]
    y_high.append(remote(wh4, rh4, y_send.at[9], y_recv.at[9], y_peer))

    loads[0].wait()
    loads[1].wait()
    for j in range(4):
        wlo[j] = fold(nn(ogx[own, 512 * j : 512 * (j + 1)], fl[...]), 128).astype(BF16)
    loads[2].wait()
    wlo[4] = fold(nn(ogx[own, 2048:2304], f4a[...]), 128).astype(BF16)
    for cp in loads[3:]:
        cp.start()

    @pl.when(c == 1)
    def _():
        pl.semaphore_wait(go, 1)

    @pl.when(mp == 1)
    def _():
        for dev in z_peers:
            signal(barrier, dev)

    @pl.when(mp == 3)
    def _():
        for dev in x_peers + [h_peer]:
            signal(barrier, dev)

    for cp in y_low:
        cp.start()
    sib_copy.start()
    loads[3].wait()
    for k in range(4):
        whi[k] = fold(nn(ogx[own, 512 * k : 512 * (k + 1)], fh[...]), 384).astype(BF16)
        y_high[k].start()
    loads[4].wait()
    wh4[...] = fold(nn(ogx[own, 2048:2304], f4b[...]), 128).astype(BF16)
    y_high[4].start()

    loads[5].wait()
    for t in range(0, TOK, 512):
        for b, (c0, cn) in enumerate(BLOCKS):
            lanes = slice(128 * b, 128 * (b + 1))
            hp[0, t : t + 512, lanes], hp[1, t : t + 512, lanes] = split(fold(nn(hx[t : t + 512, c0 : c0 + cn], fl[0:cn, :]), 128))

    def token_band(r0, n, tokens):
        a = stacked(fold(nn(ogx[tokens, pl.ds(r0, n)], fl[0:n, :]), 128), 0)
        hi = hp[0, tokens, :]
        return tn(a, cat((hi, hi, hp[1, tokens, :]), 0))

    def own_band(k, r0, n):
        for b, (c0, cn) in enumerate(BLOCKS):
            xh, xl = split(DECAY * fold(nn(mom_all[pl.ds(r0, n), c0 : c0 + cn], fl[0:cn, :]), 128))
            both = tn(fl[0:n, :], xh)
            band1[k, :, 128 * b : 128 * (b + 1)] = both[0:128] + both[128:256] + tn(fl[0:n, 0:128], xl)
        band1[k] += token_band(r0, n, loc)

    @pl.when(mp == 1)
    def _():
        pl.semaphore_wait(barrier, 7)

    @pl.when(mp == 3)
    def _():
        pl.semaphore_wait(barrier, 4)

    @pl.when(c == 1)
    def _():
        for dev in (sib, y_peer, diag):
            signal(know, dev)
        pl.semaphore_wait(know, 1)

    @pl.when(c == 0)
    def _():
        pl.semaphore_wait(know, 2)

    x_sends = []
    f_low = [remote(rlo.at[j, mine_c, :], rlo.at[j, mine_c, :], f_send.at[j], f_recv.at[j], sib) for j in range(5)]
    def x_done(j):
        n = 32 if j < 4 else 16
        for o in range(3):
            x_sends[3 * j + o].wait_recv()
        mine = rows(x * n, n, n)
        xs[j, 0:n, :] = band[j, mine, :] + xr[j, 0, 0:n, :] + xr[j, 1, 0:n, :] + xr[j, 2, 0:n, :]
        for q in range(n // 8):
            to = (4 * (j % 2) if j < 4 else 0) + q
            away = (to - z + 8) % 8
            cp = remote(
                xs.at[j, 8 * q : 8 * (q + 1), :],
                zr.at[j // 2, jnp.maximum(away - 1, 0)],
                z_send.at[j, q],
                z_recv.at[j // 2, jnp.maximum(away - 1, 0)],
                (to * 8 + h * 4 + x, mp),
            )
            z_sends.append((cp, away))
            pl.when(away != 0)(cp.start)

    z_sends = []
    sib_copy.wait_recv()
    for j in range(5):
        y_low[j].wait_recv()
        f_low[j].start()
        loads[6 + j].wait()
        own_band(j, 512 * j, 512 if j < 4 else 256)
        f_low[j].wait_recv()
        w = rlo[j]
        band[j] = band1[j] + tn(cat((w, w), 0), cat((hp[0, rem, :], hp[1, rem, :]), 0))
        n = 32 if j < 4 else 16
        for o in range(1, 4):
            theirs = rows(((x + o) % 4) * n, n, n)
            cp = remote(band.at[j, theirs, :], xr.at[j, o - 1, 0:n, :], x_send.at[j, o - 1], x_recv.at[j, o - 1], x_peers[o - 1])
            cp.start()
            x_sends.append(cp)
        if j >= 3:
            x_done(j - 3)

    def chunk(k, r0, n, high_ref, table, *beside):
        y_high[k].wait_recv()
        w = cat((rlo[k, mine_c, :], high_ref[...]), 1)
        ogx[yrows, r0 : r0 + n] = fold(nn(w, table[...]), n).astype(BF16)
        there = ogx.at[yrows, r0 : r0 + n]
        fwd = remote(there, there, f_send.at[5 + k], f_recv.at[5 + k], sib)
        fwd.start()
        for step in beside:
            step()
        fwd.wait_recv()
        bandf = band1[k] + token_band(r0, n, rem)
        for b, (c0, cn) in enumerate(BLOCKS):
            t1 = nn(stacked(bandf[:, 128 * b : 128 * (b + 1)], 1), kts[:, 0:cn])
            hi, lo = split(t1)
            for u in range(n // 256):
                part = slice(64 * u, 64 * (u + 1))
                ext[u, :, c0 : c0 + cn] = cat((hi[part], hi[part], lo[part]), 0)
        for u in range(n // 256):
            r = slice(r0 + 256 * u, r0 + 256 * (u + 1))
            g = tn(ogx[:, r], cat((hx[...], ext[u]), 0))
            out[r, :] = (DECAY * mom_all[r, :].astype(F32) + g).astype(BF16)
        return fwd

    for cp in loads[11:]:
        cp.wait()
    forwards = list(f_low)
    fin_sends = []

    def z_done(t):
        j = z // 4 + 2 * t if t < 2 else 4
        q = z % 4 if t < 2 else z % 2
        group = 8 * j + 2 * x + q // 2 if t < 2 else 32 + x
        half = q % 2
        first, last = (64 * group) // 36, (64 * group + 63) // 36
        there = z < 2 if t == 2 else z >= 0

        @pl.when(there)
        def _():
            total = xs[j, rows(8 * q, 8, 8), :]
            for o in range(7):
                slot = zr.at[t, o]
                remote(slot, slot, z_send.at[0, 0], z_recv.at[t, o], z_peers[0]).wait_recv()
                total = total + zr[t, o]
            zs[t] = total

        for u in range(3):
            owner = jnp.minimum(first + u, NDP - 1)
            slot = (group - (36 * owner) // 64) * 2 + half
            slot = jnp.clip(slot, 0, 3)
            goes = there & (first + u <= last)
            cp = remote(zs.at[t], fin.at[h, slot], fin_send.at[t, u], fin_recv.at[h, slot], (owner, mp))
            at_home = pltpu.make_async_copy(zs.at[t], fin.at[h, slot], fin_recv.at[h, slot])
            fin_sends.append((cp, goes & (owner != dp)))

            @pl.when(goes & (owner != dp))
            def _():
                cp.start()

            @pl.when(goes & (owner == dp))
            def _():
                at_home.start()

    def update():
        two = (36 * dp + 35) // 64 - (36 * dp) // 64
        for hh in range(2):
            for s in range(4):

                def arrived(hh=hh, s=s):
                    slot = fin.at[hh, s]
                    pltpu.make_async_copy(slot, slot, fin_recv.at[hh, s]).wait()

                if s < 2:
                    arrived()
                else:
                    pl.when(two == 1)(arrived)
        low = [fin[0, s] + fin[1, s] for s in range(4)]
        low = jnp.concatenate(low, axis=0)
        lefted = lax.dot_general(
            share[...], low, (((1,), (0,)), ((), ())), precision=lax.Precision.HIGHEST, preferred_element_type=F32
        )
        for b, (c0, cn) in enumerate(BLOCKS):
            u = nn(stacked(lefted[:, 128 * b : 128 * (b + 1)], 1), kts[:, 0:cn])
            upd[:, c0 : c0 + cn] = u[0:SHARE].astype(BF16)

    forwards.append(chunk(0, 0, 512, rhi.at[0], i8, lambda: x_done(2)))
    forwards.append(chunk(1, 512, 512, rhi.at[1], i8, lambda: x_done(3), lambda: x_done(4)))
    forwards.append(chunk(2, 1024, 512, rhi.at[2], i8, lambda: z_done(0), lambda: z_done(1)))
    forwards.append(chunk(3, 1536, 512, rhi.at[3], i8, lambda: z_done(2)))
    forwards.append(chunk(4, 2048, 256, rh4, i4, update))

    sib_copy.wait_send()
    for cp in y_low + y_high + forwards + x_sends:
        cp.wait_send()
    for cp, away in z_sends:
        pl.when(away != 0)(cp.wait_send)
    for cp, goes in fin_sends:
        pl.when(goes)(cp.wait_send)


def body(hidden, out_grad, momentum):
    consts = tables()
    hbm = pl.BlockSpec(memory_space=pltpu.HBM)
    vmem = pl.BlockSpec(memory_space=pltpu.VMEM)
    dma = pltpu.SemaphoreType.DMA
    return pl.pallas_call(
        kernel,
        out_shape=(pltpu.VMEM((D_WIN, COLS), BF16), pltpu.VMEM((SHARE, COLS), BF16)),
        in_specs=[hbm] * (3 + len(consts)),
        out_specs=(vmem, vmem),
        scratch_shapes=[
            *[pltpu.VMEM(t.shape, BF16) for t in consts[:7]],
            pltpu.VMEM((PADDED_SHARE, 2 * BAND), F32),
            pltpu.VMEM((TOK + 192, D_WIN), BF16),
            pltpu.VMEM((TOK, COLS), BF16),
            pltpu.VMEM((2, 192, COLS), BF16),
            pltpu.VMEM((D_WIN, COLS), BF16),
            pltpu.VMEM((5, QTOK, 128), BF16),
            pltpu.VMEM((4, QTOK, 384), BF16),
            pltpu.VMEM((QTOK, 128), BF16),
            pltpu.VMEM((5, HALF_TOK, 128), BF16),
            pltpu.VMEM((4, QTOK, 384), BF16),
            pltpu.VMEM((QTOK, 128), BF16),
            pltpu.VMEM((2, TOK, BW), BF16),
            pltpu.VMEM((5, 128, BW), F32),
            pltpu.VMEM((5, 128, BW), F32),
            pltpu.VMEM((5, 3, 32, BW), F32),
            pltpu.VMEM((5, 32, BW), F32),
            pltpu.VMEM((3, 7, 8, BW), F32),
            pltpu.VMEM((3, 8, BW), F32),
            pltpu.VMEM((2, 4, 8, BW), F32),
            dma((24,)), dma((10,)), dma((10,)), dma((10,)), dma((10,)), dma, dma,
            dma((5, 3)), dma((5, 3)), dma((5, 4)), dma((3, 7)), dma((3, 3)), dma((2, 4)),
            pltpu.SemaphoreType.REGULAR, pltpu.SemaphoreType.REGULAR,
        ],
        compiler_params=pltpu.CompilerParams(
            collective_id=0, has_side_effects=True, vmem_limit_bytes=54 * 2**20
        ),
        cost_estimate=pl.CostEstimate(flops=4 * 2 * TOK * D_WIN * COLS, bytes_accessed=16 * 2**20, transcendentals=0),
    )(hidden, out_grad, momentum, *consts)


def solution(mesh):
    return jax.shard_map(
        body,
        mesh=mesh,
        in_specs=(P("dp", "mp"), P(("dp", "mp"), None), P("dp", "mp")),
        out_specs=(P("dp", "mp"), P("dp", "mp")),
        check_vma=False,
    )
```

time: 66.5 us -> 49.5 us (0.74)
  Pallas kernels: 62.3 us -> 45.7 us
    pallas_call x1, Pallas kernels: 62.3 us -> 45.7 us  [body(): pl.pallas_call(kernel, out_shape=(pltpu.VMEM((D_WIN, COLS), BF16), pltpu....]
where the time goes in v2:
time: 49.5 us; the launch traced here: 49.3 us
  Pallas kernels  45.7 us (92%)
  local copies, waits for them, and re-layouts  3.02 us (6%)
  between operations  0.64 us (1%)
    pallas_call x1, Pallas kernels, body(): pl.pallas_call(kernel, out_shape=(pltpu.VMEM((D_WIN, COLS), BF16), pltpu....  45.7 us
    unnamed x2, local copies, waits for them, and re-layouts  3.02 us

profile of v2, /device:TPU:1, one launch (start us, length us, event | category | flops | bytes accessed | tf_op | source)
XLA Modules:
  0.0 49.3 jit_solution(2078676221185389513)
XLA Ops:
  0.6 45.7 %shard_map.131 = (bf16[2304,1152]{1,0:T(8,128)(2,1)S(1)}, bf16[36,1152]{1,0:T(8,128)(2,1)S(1)}) custom-call(bf16[1024,1152]{1,0:T(8,128)(2,1)} %hid.1, bf16[256,2304]{1,0:T(8,128)(2,1)} %og.1, bf16[2304,1152]{1,0:T(8,128)(2,1)} %mom.1, bf16[512,256]{1,0:T(8,128)(2,1)} %constant.18.clone.fl_in, bf16[512,768]{1,0:T(8,128)(2,1)} %constant.19.clone.fh_in, ...), custom_call_target="tpu_custom_call" | custom-call | flops 21743271936 | bytes 16777216 | tf_op jit(solution)/shard_map/pallas_call | solution.py:377
  46.3 2.4 %copy.16 = bf16[2304,1152]{1,0:T(8,128)(2,1)} copy(bf16[2304,1152]{1,0:T(8,128)(2,1)S(1)} %get-tuple-element.2) | data formatting | bytes 10616832
  48.7 0.6 %copy.17 = bf16[36,1152]{1,0:T(8,128)(2,1)} copy(bf16[36,1152]{1,0:T(8,128)(2,1)S(1)} %get-tuple-element.3) | data formatting | bytes 165888

commit v3 on v2

--- a/solution.py
+++ b/solution.py
@@ -102,7 +102,7 @@
 def kernel(
     hid, og, mom, fl_in, fh_in, f4a_in, f4b_in, i8_in, i4_in, kts_in, fts_in, share_in,
     out, upd,
-    fl, fh, f4a, f4b, i8, i4, kts, share, ogx, hx, ext, mom_all, wlo, whi, wh4, rlo, rhi, rh4,
+    fl, fh, f4a, f4b, i8, i4, kts, share, ogx, hx, ext, mom_all, acc, wlo, whi, wh4, rlo, rhi, rh4,
     hp, band1, band, xr, xs, zr, zs, fin,
     l_sem, y_send, y_recv, f_send, f_recv, s_send, s_recv, x_send, x_recv, z_send, z_recv, fin_send, fin_recv, go, know,
 ):
@@ -142,12 +142,13 @@
         def _():
             signal(barrier, (dp, first_core))
 
-    pairs = [(og, ogx.at[own, :]), (fl_in, fl), (f4a_in, f4a), (fh_in, fh), (f4b_in, f4b), (hid, hx.at[0:TOK, :])]
+    pairs = [(og.at[:, 0:512], ogx.at[own, 0:512]), (fl_in, fl), (f4a_in, f4a), (fh_in, fh), (f4b_in, f4b), (hid, hx.at[0:TOK, :])]
     pairs += [(mom.at[512 * k : min(512 * (k + 1), D_WIN), :], mom_all.at[512 * k : min(512 * (k + 1), D_WIN), :]) for k in range(5)]
     pairs += [(i8_in, i8), (i4_in, i4), (kts_in, kts), (share_in.at[dp], share)]
     pairs += [(fts_in, ogx.at[TOK : TOK + 192, 256 * k : 256 * (k + 1)]) for k in range(9)]
+    pairs += [(og.at[:, 512:], ogx.at[own, 512:])]
     loads = [pltpu.make_async_copy(a, b, l_sem.at[i]) for i, (a, b) in enumerate(pairs)]
-    for cp in loads[:3]:
+    for cp in loads[0:2] + loads[24:] + loads[2:4]:
         cp.start()
 
     @pl.when(c == 0)
@@ -156,22 +157,53 @@
         signal(go, sib)
 
     sib_copy = remote(og, ogx.at[own, :], s_send, s_recv, sib)
-    y_low = [remote(wlo.at[j], rlo.at[j, mine_c, :], y_send.at[j], y_recv.at[j], y_peer) for j in range(5)]
-    y_high = [remote(whi.at[k], rhi.at[k], y_send.at[5 + k], y_recv.at[5 + k], y_peer) for k in range(4)]
-    y_high.append(remote(wh4, rh4, y_send.at[9], y_recv.at[9], y_peer))
+    def y_low(j):
+        return remote(wlo.at[j], rlo.at[j, mine_c, :], y_send.at[j], y_recv.at[j], y_peer)
+
+    def y_high(k):
+        a, b = (wh4, rh4) if isinstance(k, int) and k == 4 else (whi.at[k], rhi.at[k])
+        return remote(a, b, y_send.at[5 + k], y_recv.at[5 + k], y_peer)
+
+    def f_low(j):
+        there = rlo.at[j, mine_c, :]
+        return remote(there, there, f_send.at[j], f_recv.at[j], sib)
+
+    def f_high(k, n):
+        there = ogx.at[yrows, pl.ds(first_row(k), n)]
+        return remote(there, there, f_send.at[5 + k], f_recv.at[5 + k], sib)
+
+    def x_copy(j, o, n):
+        theirs = rows(((x + o) % 4) * n, n, n)
+        return remote(band.at[j, theirs, :], xr.at[j, o - 1, 0:n, :], x_send.at[j, o - 1], x_recv.at[j, o - 1], x_peers[o - 1])
+
+    def first_row(k):
+        return 512 * k if isinstance(k, int) else pl.multiple_of(512 * k, 512)
+
+    def loop(first, last, step):
+        def once(i, carry):
+            step(i)
+            return carry
+
+        lax.fori_loop(first, last, once, 0)
+
+    def low_rows(j):
+        wlo[j] = fold(nn(ogx[own, pl.ds(first_row(j), 512)], fl[...]), 128).astype(BF16)
+        y_low(j).start()
+
+    @pl.when(c == 1)
+    def _():
+        pl.semaphore_wait(go, 1)
 
     loads[0].wait()
     loads[1].wait()
-    for j in range(4):
-        wlo[j] = fold(nn(ogx[own, 512 * j : 512 * (j + 1)], fl[...]), 128).astype(BF16)
+    loads[24].wait()
+    loop(0, 4, low_rows)
     loads[2].wait()
     wlo[4] = fold(nn(ogx[own, 2048:2304], f4a[...]), 128).astype(BF16)
-    for cp in loads[3:]:
+    y_low(4).start()
+    sib_copy.start()
+    for cp in loads[4:24]:
         cp.start()
-
-    @pl.when(c == 1)
-    def _():
-        pl.semaphore_wait(go, 1)
 
     @pl.when(mp == 1)
     def _():
@@ -183,22 +215,24 @@
         for dev in x_peers + [h_peer]:
             signal(barrier, dev)
 
-    for cp in y_low:
-        cp.start()
-    sib_copy.start()
     loads[3].wait()
-    for k in range(4):
-        whi[k] = fold(nn(ogx[own, 512 * k : 512 * (k + 1)], fh[...]), 384).astype(BF16)
-        y_high[k].start()
+    def high_rows(k):
+        whi[k] = fold(nn(ogx[own, pl.ds(first_row(k), 512)], fh[...]), 384).astype(BF16)
+        y_high(k).start()
+
+    loop(0, 4, high_rows)
     loads[4].wait()
     wh4[...] = fold(nn(ogx[own, 2048:2304], f4b[...]), 128).astype(BF16)
-    y_high[4].start()
+    y_high(4).start()
 
     loads[5].wait()
-    for t in range(0, TOK, 512):
+    def hidden_band(i):
+        t = rows(512 * i, 512, 512)
         for b, (c0, cn) in enumerate(BLOCKS):
             lanes = slice(128 * b, 128 * (b + 1))
-            hp[0, t : t + 512, lanes], hp[1, t : t + 512, lanes] = split(fold(nn(hx[t : t + 512, c0 : c0 + cn], fl[0:cn, :]), 128))
+            hp[0, t, lanes], hp[1, t, lanes] = split(fold(nn(hx[t, c0 : c0 + cn], fl[0:cn, :]), 128))
+
+    loop(0, 2, hidden_band)
 
     def token_band(r0, n, tokens):
         a = stacked(fold(nn(ogx[tokens, pl.ds(r0, n)], fl[0:n, :]), 128), 0)
@@ -212,6 +246,50 @@
             band1[k, :, 128 * b : 128 * (b + 1)] = both[0:128] + both[128:256] + tn(fl[0:n, 0:128], xl)
         band1[k] += token_band(r0, n, loc)
 
+    def z_copy(j, q):
+        to = (4 * (j % 2) if j < 4 else 0) + q
+        away = (to - z + 8) % 8
+        cp = remote(
+            xs.at[j, 8 * q : 8 * (q + 1), :],
+            zr.at[j // 2, jnp.maximum(away - 1, 0)],
+            z_send.at[j, q],
+            z_recv.at[j // 2, jnp.maximum(away - 1, 0)],
+            (to * 8 + h * 4 + x, mp),
+        )
+        return cp, away
+
+    def x_done(j):
+        n = 32 if j < 4 else 16
+        for o in range(3):
+            x_copy(j, o + 1, n).wait_recv()
+        mine = rows(x * n, n, n)
+        xs[j, 0:n, :] = band[j, mine, :] + xr[j, 0, 0:n, :] + xr[j, 1, 0:n, :] + xr[j, 2, 0:n, :]
+        for q in range(n // 8):
+            cp, away = z_copy(j, q)
+            pl.when(away != 0)(cp.start)
+
+    sib_copy.wait_recv()
+    for k in range(5):
+        loads[6 + k].wait()
+
+    def own_step(j, n=512):
+        y_low(j).wait_recv()
+        f_low(j).start()
+        own_band(j, first_row(j), n)
+
+    def send_step(j, n=512):
+        f_low(j).wait_recv()
+        w = rlo[j]
+        band[j] = band1[j] + tn(cat((w, w), 0), cat((hp[0, rem, :], hp[1, rem, :]), 0))
+        for o in range(1, 4):
+            x_copy(j, o, n // 16).start()
+
+    def both(j):
+        own_step(j)
+        send_step(j)
+
+    loop(0, 2, own_step)
+
     @pl.when(mp == 1)
     def _():
         pl.semaphore_wait(barrier, 7)
@@ -230,81 +308,56 @@
     def _():
         pl.semaphore_wait(know, 2)
 
-    x_sends = []
-    f_low = [remote(rlo.at[j, mine_c, :], rlo.at[j, mine_c, :], f_send.at[j], f_recv.at[j], sib) for j in range(5)]
-    def x_done(j):
-        n = 32 if j < 4 else 16
-        for o in range(3):
-            x_sends[3 * j + o].wait_recv()
-        mine = rows(x * n, n, n)
-        xs[j, 0:n, :] = band[j, mine, :] + xr[j, 0, 0:n, :] + xr[j, 1, 0:n, :] + xr[j, 2, 0:n, :]
-        for q in range(n // 8):
-            to = (4 * (j % 2) if j < 4 else 0) + q
-            away = (to - z + 8) % 8
-            cp = remote(
-                xs.at[j, 8 * q : 8 * (q + 1), :],
-                zr.at[j // 2, jnp.maximum(away - 1, 0)],
-                z_send.at[j, q],
-                z_recv.at[j // 2, jnp.maximum(away - 1, 0)],
-                (to * 8 + h * 4 + x, mp),
-            )
-            z_sends.append((cp, away))
-            pl.when(away != 0)(cp.start)
-
-    z_sends = []
-    sib_copy.wait_recv()
-    for j in range(5):
-        y_low[j].wait_recv()
-        f_low[j].start()
-        loads[6 + j].wait()
-        own_band(j, 512 * j, 512 if j < 4 else 256)
-        f_low[j].wait_recv()
-        w = rlo[j]
-        band[j] = band1[j] + tn(cat((w, w), 0), cat((hp[0, rem, :], hp[1, rem, :]), 0))
-        n = 32 if j < 4 else 16
-        for o in range(1, 4):
-            theirs = rows(((x + o) % 4) * n, n, n)
-            cp = remote(band.at[j, theirs, :], xr.at[j, o - 1, 0:n, :], x_send.at[j, o - 1], x_recv.at[j, o - 1], x_peers[o - 1])
-            cp.start()
-            x_sends.append(cp)
-        if j >= 3:
-            x_done(j - 3)
-
-    def chunk(k, r0, n, high_ref, table, *beside):
-        y_high[k].wait_recv()
-        w = cat((rlo[k, mine_c, :], high_ref[...]), 1)
-        ogx[yrows, r0 : r0 + n] = fold(nn(w, table[...]), n).astype(BF16)
-        there = ogx.at[yrows, r0 : r0 + n]
-        fwd = remote(there, there, f_send.at[5 + k], f_recv.at[5 + k], sib)
-        fwd.start()
-        for step in beside:
-            step()
-        fwd.wait_recv()
-        bandf = band1[k] + token_band(r0, n, rem)
+    loop(0, 2, send_step)
+    loop(2, 4, both)
+    own_step(4, 256)
+    send_step(4, 256)
+
+    def arrive(k, n, table):
+        y_high(k).wait_recv()
+        w = cat((rlo[k, mine_c, :], rhi[k] if n == 512 else rh4[...]), 1)
+        ogx[yrows, pl.ds(first_row(k), n)] = fold(nn(w, table[...]), n).astype(BF16)
+        f_high(k, n).start()
+
+    def extend(k):
         for b, (c0, cn) in enumerate(BLOCKS):
-            t1 = nn(stacked(bandf[:, 128 * b : 128 * (b + 1)], 1), kts[:, 0:cn])
+            t1 = nn(stacked(band[k, :, 128 * b : 128 * (b + 1)], 1), kts[:, 0:cn])
             hi, lo = split(t1)
-            for u in range(n // 256):
+            for u in range(2):
                 part = slice(64 * u, 64 * (u + 1))
                 ext[u, :, c0 : c0 + cn] = cat((hi[part], hi[part], lo[part]), 0)
-        for u in range(n // 256):
-            r = slice(r0 + 256 * u, r0 + 256 * (u + 1))
-            g = tn(ogx[:, r], cat((hx[...], ext[u]), 0))
-            out[r, :] = (DECAY * mom_all[r, :].astype(F32) + g).astype(BF16)
-        return fwd
-
-    for cp in loads[11:]:
+
+    def own_part(u, i):
+        r = rows(256 * u, 256, 256)
+        g = tn(cat((ogx[loc, r], ogx[TOK : TOK + 192, r]), 0), cat((hx[loc, :], ext[i]), 0))
+        acc[r, :] = DECAY * mom_all[r, :].astype(F32) + g
+
+    def fresh(u):
+        r = rows(256 * u, 256, 256)
+        out[r, :] = (acc[r, :] + tn(ogx[rem, r], hx[rem, :])).astype(BF16)
+
+    for cp in loads[11:24]:
         cp.wait()
-    forwards = list(f_low)
-    fin_sends = []
-
-    def z_done(t):
+    def piece(t):
         j = z // 4 + 2 * t if t < 2 else 4
         q = z % 4 if t < 2 else z % 2
         group = 8 * j + 2 * x + q // 2 if t < 2 else 32 + x
         half = q % 2
         first, last = (64 * group) // 36, (64 * group + 63) // 36
         there = z < 2 if t == 2 else z >= 0
+        return j, q, group, half, first, last, there
+
+    def fin_copy(t, u):
+        j, q, group, half, first, last, there = piece(t)
+        owner = jnp.minimum(first + u, NDP - 1)
+        slot = jnp.clip((group - (36 * owner) // 64) * 2 + half, 0, 3)
+        goes = there & (first + u <= last)
+        cp = remote(zs.at[t], fin.at[h, slot], fin_send.at[t, u], fin_recv.at[h, slot], (owner, mp))
+        at_home = pltpu.make_async_copy(zs.at[t], fin.at[h, slot], fin_recv.at[h, slot])
+        return cp, at_home, goes & (owner != dp), goes & (owner == dp)
+
+    def z_done(t):
+        j, q, group, half, first, last, there = piece(t)
 
         @pl.when(there)
         def _():
@@ -316,21 +369,9 @@
             zs[t] = total
 
         for u in range(3):
-            owner = jnp.minimum(first + u, NDP - 1)
-            slot = (group - (36 * owner) // 64) * 2 + half
-            slot = jnp.clip(slot, 0, 3)
-            goes = there & (first + u <= last)
-            cp = remote(zs.at[t], fin.at[h, slot], fin_send.at[t, u], fin_recv.at[h, slot], (owner, mp))
-            at_home = pltpu.make_async_copy(zs.at[t], fin.at[h, slot], fin_recv.at[h, slot])
-            fin_sends.append((cp, goes & (owner != dp)))
-
-            @pl.when(goes & (owner != dp))
-            def _():
-                cp.start()
-
-            @pl.when(goes & (owner == dp))
-            def _():
-                at_home.start()
+            cp, at_home, away, here = fin_copy(t, u)
+            pl.when(away)(cp.start)
+            pl.when(here)(at_home.start)
 
     def update():
         two = (36 * dp + 35) // 64 - (36 * dp) // 64
@@ -354,19 +395,63 @@
             u = nn(stacked(lefted[:, 128 * b : 128 * (b + 1)], 1), kts[:, 0:cn])
             upd[:, c0 : c0 + cn] = u[0:SHARE].astype(BF16)
 
-    forwards.append(chunk(0, 0, 512, rhi.at[0], i8, lambda: x_done(2)))
-    forwards.append(chunk(1, 512, 512, rhi.at[1], i8, lambda: x_done(3), lambda: x_done(4)))
-    forwards.append(chunk(2, 1024, 512, rhi.at[2], i8, lambda: z_done(0), lambda: z_done(1)))
-    forwards.append(chunk(3, 1536, 512, rhi.at[3], i8, lambda: z_done(2)))
-    forwards.append(chunk(4, 2048, 256, rh4, i4, update))
+    def chunk(k):
+        arrive(k, 512, i8)
+        extend(k)
+        loop(0, 2, lambda i: own_part(2 * k + i, i))
+
+        @pl.when(k == 0)
+        def _():
+            x_done(0)
+            x_done(1)
+
+        @pl.when(k == 1)
+        def _():
+            x_done(2)
+            x_done(3)
+
+        f_high(k, 512).wait_recv()
+        fresh(2 * k)
+
+        @pl.when(k == 3)
+        def _():
+            arrive(4, 256, i4)
+
+        fresh(2 * k + 1)
+
+        @pl.when(k == 1)
+        def _():
+            x_done(4)
+            z_done(0)
+
+        @pl.when(k == 2)
+        def _():
+            extend(4)
+            own_part(8, 0)
+            z_done(1)
+            z_done(2)
+
+    loop(0, 4, chunk)
+    update()
+    f_high(4, 256).wait_recv()
+    fresh(8)
 
     sib_copy.wait_send()
-    for cp in y_low + y_high + forwards + x_sends:
-        cp.wait_send()
-    for cp, away in z_sends:
-        pl.when(away != 0)(cp.wait_send)
-    for cp, goes in fin_sends:
-        pl.when(goes)(cp.wait_send)
+    for k in range(5):
+        y_low(k).wait_send()
+        y_high(k).wait_send()
+        f_low(k).wait_send()
+        f_high(k, 512 if k < 4 else 256).wait_send()
+        for o in range(1, 4):
+            x_copy(k, o, 32 if k < 4 else 16).wait_send()
+    for j in range(5):
+        for q in range(4 if j < 4 else 2):
+            cp, away = z_copy(j, q)
+            pl.when(away != 0)(cp.wait_send)
+    for t in range(3):
+        for u in range(3):
+            cp, at_home, away, here = fin_copy(t, u)
+            pl.when(away)(cp.wait_send)
 
 
 def body(hidden, out_grad, momentum):
@@ -386,6 +471,7 @@
             pltpu.VMEM((TOK, COLS), BF16),
             pltpu.VMEM((2, 192, COLS), BF16),
             pltpu.VMEM((D_WIN, COLS), BF16),
+            pltpu.VMEM((D_WIN, COLS), F32),
             pltpu.VMEM((5, QTOK, 128), BF16),
             pltpu.VMEM((4, QTOK, 384), BF16),
             pltpu.VMEM((QTOK, 128), BF16),
@@ -400,7 +486,7 @@
             pltpu.VMEM((3, 7, 8, BW), F32),
             pltpu.VMEM((3, 8, BW), F32),
             pltpu.VMEM((2, 4, 8, BW), F32),
-            dma((24,)), dma((10,)), dma((10,)), dma((10,)), dma((10,)), dma, dma,
+            dma((25,)), dma((10,)), dma((10,)), dma((10,)), dma((10,)), dma, dma,
             dma((5, 3)), dma((5, 3)), dma((5, 4)), dma((3, 7)), dma((3, 3)), dma((2, 4)),
             pltpu.SemaphoreType.REGULAR, pltpu.SemaphoreType.REGULAR,
         ],

time: 49.5 us -> 46.3 us (0.935)
  Pallas kernels: 45.7 us -> 42.4 us
    pallas_call x1, Pallas kernels: 45.7 us -> 42.4 us  [body(): pl.pallas_call(kernel, out_shape=(pltpu.VMEM((D_WIN, COLS), BF16), pltpu....]
where the time goes in v3:
time: 46.3 us; the launch traced here: 46.1 us
  Pallas kernels  42.4 us (92%)
  local copies, waits for them, and re-layouts  3.02 us (7%)
  between operations  0.64 us (1%)
    pallas_call x1, Pallas kernels, body(): pl.pallas_call(kernel, out_shape=(pltpu.VMEM((D_WIN, COLS), BF16), pltpu....  42.4 us
    unnamed x2, local copies, waits for them, and re-layouts  3.02 us

profile of v3, /device:TPU:1, one launch (start us, length us, event | category | flops | bytes accessed | tf_op | source)
XLA Modules:
  0.0 46.1 jit_solution(8987361170751171504)
XLA Ops:
  0.6 42.4 %shard_map.131 = (bf16[2304,1152]{1,0:T(8,128)(2,1)S(1)}, bf16[36,1152]{1,0:T(8,128)(2,1)S(1)}) custom-call(bf16[1024,1152]{1,0:T(8,128)(2,1)} %hid.1, bf16[256,2304]{1,0:T(8,128)(2,1)} %og.1, bf16[2304,1152]{1,0:T(8,128)(2,1)} %mom.1, bf16[512,256]{1,0:T(8,128)(2,1)} %constant.18.clone.fl_in, bf16[512,768]{1,0:T(8,128)(2,1)} %constant.19.clone.fh_in, ...), custom_call_target="tpu_custom_call" | custom-call | flops 21743271936 | bytes 16777216 | tf_op jit(solution)/shard_map/pallas_call | solution.py:462
  43.1 2.4 %copy.16 = bf16[2304,1152]{1,0:T(8,128)(2,1)} copy(bf16[2304,1152]{1,0:T(8,128)(2,1)S(1)} %get-tuple-element.2) | data formatting | bytes 10616832
  45.4 0.6 %copy.17 = bf16[36,1152]{1,0:T(8,128)(2,1)} copy(bf16[36,1152]{1,0:T(8,128)(2,1)S(1)} %get-tuple-element.3) | data formatting | bytes 165888

commit v4 on v3

--- a/solution.py
+++ b/solution.py
@@ -409,6 +409,14 @@
         def _():
             x_done(2)
             x_done(3)
+            x_done(4)
+
+        @pl.when(k == 2)
+        def _():
+            z_done(0)
+            z_done(1)
+            extend(4)
+            own_part(8, 0)
 
         f_high(k, 512).wait_recv()
         fresh(2 * k)
@@ -419,16 +427,8 @@
 
         fresh(2 * k + 1)
 
-        @pl.when(k == 1)
-        def _():
-            x_done(4)
-            z_done(0)
-
         @pl.when(k == 2)
         def _():
-            extend(4)
-            own_part(8, 0)
-            z_done(1)
             z_done(2)
 
     loop(0, 4, chunk)

time: 46.3 us -> 46.6 us (level)
  Pallas kernels: 42.4 us -> 42.9 us
where the time goes in v4:
time: 46.6 us; the launch traced here: 46.5 us
  Pallas kernels  42.9 us (92%)
  local copies, waits for them, and re-layouts  3.02 us (6%)
  between operations  0.64 us (1%)
    pallas_call x1, Pallas kernels, body(): pl.pallas_call(kernel, out_shape=(pltpu.VMEM((D_WIN, COLS), BF16), pltpu....  42.9 us
    unnamed x2, local copies, waits for them, and re-layouts  3.02 us

profile of v4, /device:TPU:1, one launch (start us, length us, event | category | flops | bytes accessed | tf_op | source)
XLA Modules:
  0.0 46.5 jit_solution(15653636750369221387)
XLA Ops:
  0.6 42.9 %shard_map.131 = (bf16[2304,1152]{1,0:T(8,128)(2,1)S(1)}, bf16[36,1152]{1,0:T(8,128)(2,1)S(1)}) custom-call(bf16[1024,1152]{1,0:T(8,128)(2,1)} %hid.1, bf16[256,2304]{1,0:T(8,128)(2,1)} %og.1, bf16[2304,1152]{1,0:T(8,128)(2,1)} %mom.1, bf16[512,256]{1,0:T(8,128)(2,1)} %constant.18.clone.fl_in, bf16[512,768]{1,0:T(8,128)(2,1)} %constant.19.clone.fh_in, ...), custom_call_target="tpu_custom_call" | custom-call | flops 21743271936 | bytes 16777216 | tf_op jit(solution)/shard_map/pallas_call | solution.py:462
  43.5 2.4 %copy.16 = bf16[2304,1152]{1,0:T(8,128)(2,1)} copy(bf16[2304,1152]{1,0:T(8,128)(2,1)S(1)} %get-tuple-element.2) | data formatting | bytes 10616832
  45.9 0.6 %copy.17 = bf16[36,1152]{1,0:T(8,128)(2,1)} copy(bf16[36,1152]{1,0:T(8,128)(2,1)S(1)} %get-tuple-element.3) | data formatting | bytes 165888
